TPU v7x, 32 devices: a whole 2x2x4 slice. The times are simulated.
32 devices in a mesh: layer: 4 (over z), row: 8 (over y, x, core).
Axes of the slice: x: 2, y: 2, z: 4, core: 2. Of those that a mesh axis runs over, the one named last changes fastest.
Arguments:
- tile_left: bfloat16 [48, 4, 64, 1024], P('row', 'layer'), may hold values from -6 to 6
- tile_right: bfloat16 [48, 4, 64, 1024], P('row', 'layer'), may hold values from -0.1875 to 0.1875
- tile_mask: int32 [48, 4], P('row', 'layer'), may hold values from 0 to 1, as said below
- orig_left: bfloat16 [48, 64, 1024], P('row'), may hold values from -6 to 6
- orig_right: bfloat16 [48, 64, 1024], P('row'), may hold values from -0.75 to 0.75
- pivot_left: bfloat16 [4, 64, 1024], P('layer', None, 'row'), may hold values from -6 to 6
- pivot_right: bfloat16 [4, 64, 1024], P('layer', None, 'row'), may hold values from -0.1875 to 0.1875
- sketch: bfloat16 [64, 1024], replicated, may hold values from -0.1875 to 0.1875
- pivot_factor: float32 [1024, 1024], P(('layer', 'row')), as said below
Outputs:
- solved_factor: float32 [48, 64, 1024], P('row')
Inputs may be any that keep to these rules, and one draw needn't show every extreme that they name: `tile_mask`: every tile row is updated by at least one earlier panel. `pivot_factor`: lower triangular with a positive diagonal.
All inputs are finite; a program needn't handle non-finite values.
Results may differ from a plain program's by a relative error of at most 0.0003.
Values may be sent and summed in bfloat16 or wider, within the bound.
A program may use at most 64 MiB of HBM per device.

v0:
```python
from functools import partial

import jax
import jax.numpy as jnp
from jax import lax
from jax.sharding import PartitionSpec as P


def solve_rows(pivot_whole, core):
    tile_count, rank_rows, cell_count = core.shape
    right_sides = core.reshape(tile_count * rank_rows, cell_count).T
    solution = jax.scipy.linalg.solve_triangular(pivot_whole, right_sides, lower=True)
    return solution.T.reshape(tile_count, rank_rows, cell_count)


def shards(
    tile_left,
    tile_right,
    tile_mask,
    orig_left,
    orig_right,
    pivot_left,
    pivot_right,
    sketch,
    pivot_factor,
):
    highest = lax.Precision.HIGHEST
    pivot_whole = lax.all_gather(pivot_factor, ("layer", "row"), axis=0, tiled=True)
    left_whole, right_whole = (
        lax.all_gather(pivot_left, "row", axis=2, tiled=True),
        lax.all_gather(pivot_right, "row", axis=2, tiled=True),
    )
    coupling = jnp.einsum(
        "tpqb,psb->tpqs", tile_right, right_whole, preferred_element_type=jnp.float32
    )
    weights = tile_mask.astype(jnp.float32)[:, :, None, None]
    update_left = (
        jnp.einsum("tpqs,tpqb->tpsb", coupling, tile_left.astype(jnp.float32), precision=highest)
        * weights
    )
    sketched = jnp.einsum("pqb,sb->pqs", left_whole, sketch, preferred_element_type=jnp.float32)
    partial_sample = jnp.einsum("tpqb,pqs->tsb", update_left, sketched, precision=highest)
    orig_float = orig_left.astype(jnp.float32)
    orig_sketch = jnp.einsum("tqb,sb->tqs", orig_right, sketch, preferred_element_type=jnp.float32)
    own_sample = jnp.einsum("tqb,tqs->tsb", orig_float, orig_sketch, precision=highest)
    sample = own_sample - lax.psum(partial_sample, "layer")
    gram_matrix = jnp.einsum("tqb,tsb->tqs", sample, sample, precision=highest)
    factor = jnp.linalg.cholesky(gram_matrix)
    row_basis = jax.vmap(partial(jax.scipy.linalg.solve_triangular, lower=True))(factor, sample)
    projected = jnp.einsum("tpqb,tsb->tpqs", update_left, row_basis, precision=highest)
    partial_core = jnp.einsum(
        "pqb,tpqs->tsb", left_whole.astype(jnp.float32), projected, precision=highest
    )
    orig_basis = jnp.einsum("tqb,tsb->tqs", orig_float, row_basis, precision=highest)
    own_core = jnp.einsum(
        "tqb,tqs->tsb", orig_right.astype(jnp.float32), orig_basis, precision=highest
    )
    joined = lax.psum(partial_core, "layer")
    return solve_rows(pivot_whole, own_core - joined)


def solution(mesh):
    in_specs = (
        P("row", "layer", None, None),
        P("row", "layer", None, None),
        P("row", "layer"),
        P("row", None, None),
        P("row", None, None),
        P("layer", None, "row"),
        P("layer", None, "row"),
        P(),
        P(("layer", "row"), None),
    )
    out_specs = P("row", None, None)
    return jax.shard_map(shards, mesh=mesh, in_specs=in_specs, out_specs=out_specs, check_vma=False)
```

profile of v0, /device:TPU:1, one launch (start us, length us, event | category | flops | bytes accessed | tf_op | source)
XLA Modules:
  0.0 417.5 jit_solution(10956328244340226833)
XLA Ops:
  8.2 10.6 %all_gather.10 = bf16[1,64,1024]{2,1,0:T(8,128)(2,1)S(1)} all-gather(bf16[1,64,128]{2,1,0:T(8,128)(2,1)} %param.14), channel_id=1, replica_groups=mesh['layer'=4,'row'=8] {'row'}, dimensions={2}, use_global_device_ids=true | all-gather | bytes 147456 | tf_op jit(solution)/shard_map/all_gather | solution.py:30
  18.7 8.9 %all_gather.11 = bf16[1,64,1024]{2,1,0:T(8,128)(2,1)S(1)} all-gather(bf16[1,64,128]{2,1,0:T(8,128)(2,1)} %param.15), channel_id=1, replica_groups=mesh['layer'=4,'row'=8] {'row'}, dimensions={2}, use_global_device_ids=true | all-gather | bytes 147456 | tf_op jit(solution)/shard_map/all_gather | solution.py:31
  28.7 1.6 convolution_bitcast_fusion.1
  32.2 2.6 convolution_bitcast_fusion
  36.5 66.3 %all-reduce.3.cloned.1.call-done = f32[6,64,1024]{2,1,0:T(8,128)} async-done(((f32[6,64,1024]{2,1,0:T(8,128)}), f32[6,64,1024]{2,1,0:T(8,128)}) %all-reduce.3.cloned.1.call-update) | async-done | bytes 1572880 | tf_op jit(solution)/shard_map/psum | solution.py:46
  102.8 2.2 convolution_subtract_fusion.1
  105.0 1.6 fusion.46
  107.4 1.6 fusion.27
  109.0 35.9 %custom-call.13 = f32[6,64,64]{2,1,0:T(8,128)S(1)} custom-call(f32[6,64,64]{2,1,0:T(8,128)} %fusion.27), custom_call_target="Cholesky" | custom-call | tf_op jit(solution)/shard_map/jit(cholesky)/cholesky | solution.py:48
  145.9 30.2 %custom-call.14 = f32[6,1,64,64]{2,3,1,0:T(8,128)S(1)} custom-call(f32[6,1,64,64]{3,2,1,0:T(8,128)} %select_bitcast_fusion), custom_call_target="InvertDiagBlocksLowerTriangular" | custom-call | tf_op jit(solution)/shard_map/vmap(jit(_solve_triangular))/triangular_solve | solution.py:49
  177.6 1.7 fusion.48
  179.3 1.9 fusion.29
  183.5 74.1 %all-reduce.5.cloned.1.call-done = f32[6,64,1024]{2,1,0:T(8,128)} async-done(((f32[6,64,1024]{2,1,0:T(8,128)}), f32[6,64,1024]{2,1,0:T(8,128)}) %all-reduce.5.cloned.1.call-update) | async-done | bytes 1572880 | tf_op jit(solution)/shard_map/psum | solution.py:58
  257.6 2.2 convolution_subtract_fusion
  259.8 1.6 copy.21
  261.4 13.4 %all-gather.2.cloned.1.call-done = f32[1024,1024]{1,0:T(8,128)} async-done(((f32[32,1024]{1,0:T(8,128)}), f32[1024,1024]{1,0:T(8,128)}) %all-gather.2.cloned.1.call-update) | async-done | bytes 4194320 | tf_op jit(solution)/shard_map/all_gather | solution.py:28
  274.7 4.7 %fusion = f32[1024,1024]{1,0:T(8,128)} fusion(f32[1024,1024]{1,0:T(8,128)} %all-gather.2.cloned.1.call-done), kind=kLoop, calls=%fused_computation.3 | loop fusion | flops 2097152 | bytes 8388608 | tf_op jit(solution)/shard_map/jit(_solve_triangular)/triangular_solve | solution.py:12
  279.5 28.3 %while.1 = (s32[]{:T(128)}, f32[1024,1024]{1,0:T(8,128)}, s32[8,2]{0,1:T(2,128)S(1)}, f32[8,128,128]{2,1,0:T(8,128)}, s32[]{:T(128)}) while((s32[]{:T(128)}, f32[1024,1024]{1,0:T(8,128)}, s32[8,2]{0,1:T(2,128)S(1)}, f32[8,128,128]{2,1,0:T(8,128)}, s32[]{:T(128)}) %tuple.41), condition=%wide.while_cond, body=%wide.while_body.sunk | while | flops 2 | bytes 132205 | solution.py:12
  280.1 2.9 bitcast_dynamic-update-slice_fusion.2
  283.7 2.9 bitcast_dynamic-update-slice_fusion.2
  287.2 2.9 bitcast_dynamic-update-slice_fusion.2
  290.8 2.9 bitcast_dynamic-update-slice_fusion.2
  294.3 2.9 bitcast_dynamic-update-slice_fusion.2
  297.9 2.9 bitcast_dynamic-update-slice_fusion.2
  301.4 2.9 bitcast_dynamic-update-slice_fusion.2
  305.0 2.8 bitcast_dynamic-update-slice_fusion.2
  307.8 79.4 %custom-call.12 = f32[8,128,128]{1,2,0:T(8,128)S(1)} custom-call(f32[8,128,128]{2,1,0:T(8,128)} %get-tuple-element.12), custom_call_target="InvertDiagBlocksLowerTriangular" | custom-call | tf_op jit(solution)/shard_map/jit(_solve_triangular)/triangular_solve | solution.py:12
  395.5 1.6 convolution_subtract_fusion.7
  398.1 1.8 convolution_subtract_fusion.8
  400.9 1.9 convolution_subtract_fusion.3
  403.9 2.1 convolution_subtract_fusion.2
  407.1 3.0 copy.22
  (66 shorter events, 28.6 us)
Async XLA Ops:
  7.4 95.5 %copy-start = (bf16[6,64,1024]{2,1,0:T(8,128)(2,1)S(1)}, bf16[6,64,1024]{2,1,0:T(8,128)(2,1)}, u32[]{:S(2)}) copy-start(bf16[6,64,1024]{2,1,0:T(8,128)(2,1)} %param.12) | copy-start | bytes 2359300
  7.4 22.9 %copy-start.7 = (bf16[6,1,64,1024]{3,2,1,0:T(8,128)(2,1)S(1)}, bf16[6,1,64,1024]{3,2,1,0:T(8,128)(2,1)}, u32[]{:S(2)}) copy-start(bf16[6,1,64,1024]{3,2,1,0:T(8,128)(2,1)} %param.9) | copy-start | bytes 2359300
  7.4 95.5 %all-reduce.3.cloned.1.call-start = ((), (), s32[]{:S(2)}) async-start(), calls=%async_computation.1 | async-start | bytes 3145728 | tf_op jit(solution)/shard_map/psum | solution.py:46
  31.1 1.1 copy-start.1
  34.8 1.1 copy-start.6
  34.9 1.1 copy-start.8
  34.9 222.7 %all-reduce.5.cloned.1.call-start = ((), (), s32[]{:S(2)}) async-start(), calls=%async_computation.2 | async-start | bytes 3145728 | tf_op jit(solution)/shard_map/psum | solution.py:58
  176.1 1.5 copy-start.2
  177.6 1.7 copy-start.3
  181.2 1.4 copy-start.4
  181.3 93.5 %all-gather.2.cloned.1.call-start = ((), (), s32[]{:S(2)}) async-start(), calls=%async_computation | async-start | bytes 4325376 | tf_op jit(solution)/shard_map/all_gather | solution.py:28
  261.4 125.8 %copy-start.5 = (f32[384,1024]{0,1:T(8,128)S(1)}, f32[384,1024]{0,1:T(8,128)}, u32[]{:S(2)}) copy-start(f32[384,1024]{0,1:T(8,128)} %copy.21) | copy-start | bytes 4718596
Sparse Core Ops, SparseCore 0:
  35.0 67.7 all-reduce.2
  181.4 76.1 all-reduce.4
Sparse Core Ops, SparseCore 1:
  184.6 90.1 all-gather.1
where the time goes:
time: 419 us; the launch traced here: 418 us
  other arithmetic  154 us (37%)
  waiting for transfers between devices  154 us (37%)
  matrix products  38.2 us (9%)
  local copies, waits for them, and re-layouts  36.7 us (9%)
  blocking collectives  19.4 us (5%)
  between operations  15.1 us (4%)
    another operation x3, other arithmetic, solve_rows(): jax.scipy.linalg.solve_triangular(pivot_whole, right_sides, lower=True)  84.1 us
    psum x1, waiting for transfers between devices, shards(): joined = lax.psum(partial_core, 'layer')  74.1 us
    psum x1, waiting for transfers between devices, shards(): sample = own_sample - lax.psum(partial_sample, 'layer')  66.3 us
    another operation x4, other arithmetic, shards(): factor = jnp.linalg.cholesky(gram_matrix)  36.1 us
    another operation x3, other arithmetic, shards(): jax.vmap(partial(jax.scipy.linalg.solve_triangular, lower=True))  31 us
    another operation x24, local copies, waits for them, and re-layouts  28.3 us
    another operation x15, matrix products, solve_rows(): jax.scipy.linalg.solve_triangular(pivot_whole, right_sides, lower=True)  19.8 us
    all_gather x1, waiting for transfers between devices, shards(): lax.all_gather(pivot_factor, ('layer', 'row'), axis=0, tiled=True)  13.4 us
  transfers between devices with their start and end apart: 3, of which 3 were waited for; matrix products, arithmetic and copies ran while one was open for 1% of the time, Pallas kernels for 0%

commit v1 on v0

v1 whole, which is shorter than its diff:
```python
from functools import partial

import jax
import jax.numpy as jnp
from jax import lax
from jax.experimental import pallas as pl
from jax.experimental.pallas import tpu as pltpu
from jax.sharding import PartitionSpec as P

HIGHEST = lax.Precision.HIGHEST
F32 = jnp.float32
BF16 = jnp.bfloat16
NN = (((1,), (0,)), ((), ()))
NT = (((1,), (1,)), ((), ()))
TN = (((0,), (0,)), ((), ()))


def dot(a, b, dims, precision=None):
    return lax.dot_general(a, b, dims, precision=precision, preferred_element_type=F32)


def split(x):
    high = x.astype(BF16)
    return high, (x - high.astype(F32)).astype(BF16)


def dot3(a, b, dims):
    (ah, al), (bh, bl) = a, b
    return dot(ah, bh, dims) + (dot(ah, bl, dims) + dot(al, bh, dims))


def owners(tiles, layers):
    base, extra = divmod(tiles, layers)
    order = sorted(range(layers), key=lambda i: abs(2 * i - layers + 1))
    count = [base + (order.index(i) < extra) for i in range(layers)]
    first = [sum(count[:i]) for i in range(layers)]
    return count, first


def pick(table, index):
    value = jnp.int32(table[0])
    for i in range(1, len(table)):
        value = jnp.where(index == i, jnp.int32(table[i]), value)
    return value


def invert_lower(block, size, stop):
    rows = lax.broadcasted_iota(jnp.int32, (size, size), 0)
    cols = lax.broadcasted_iota(jnp.int32, (size, size), 1)
    eye = rows == cols
    inverse = jnp.where(eye, 1.0 / jnp.where(eye, block, 1.0), 0.0)
    step = 1
    while step < stop:
        pair = (rows // (2 * step) == cols // (2 * step)) & (rows // step > cols // step)
        below = jnp.where(pair, block, 0.0)
        inverse = inverse - dot(inverse, dot(below, inverse, NN, HIGHEST), NN, HIGHEST)
        step *= 2
    return inverse


def eliminate(augmented, rank):
    done = []
    left = augmented
    for block in range(rank // 8):
        index = lax.broadcasted_iota(jnp.int32, (left.shape[0], left.shape[1], 1), 1)
        for at in range(8):
            column = block * 8 + at
            pivot = left[:, at : at + 1, :]
            scale = 1.0 / pivot[:, :, column : column + 1]
            weight = jnp.where(index > at, left[:, :, column : column + 1] * scale, 0.0)
            left = left - weight * pivot
        done.append(left[:, :8, :])
        left = left[:, 8:, :]
    whole = jnp.concatenate(done, axis=1)
    lanes = lax.broadcasted_iota(jnp.int32, whole.shape, 2)
    index = lax.broadcasted_iota(jnp.int32, whole.shape, 1)
    diagonal = jnp.sum(jnp.where(lanes == index, whole, 0.0), axis=2, keepdims=True)
    return whole * lax.rsqrt(diagonal)


def kernel(
    layers, rows, mask_ref, tl_ref, tr_ref, ol_ref, or_ref, pl_ref, pr_ref, sk_ref, pf_ref,
    out_ref,
    prw, plw, pw, zbuf, ce, cebuf, fbuf, mall, diag, core,
    pr_send, pr_recv, pl_send, pl_recv, pz_send, pf_send, p3_send, p_recv,
    plz_send, plf_send, tl_send, tl_recv, ce_send, ce_recv, m_send, m_recv,
):
    layer, row = lax.axis_index("layer"), lax.axis_index("row")
    tiles, rank, width = tl_ref.shape
    piece = pl_ref.shape[1]
    strip = pf_ref.shape[0]
    count, first = owners(tiles, layers)
    slots = max(count)
    chips = rows // 2
    sibling = row + 1 - 2 * lax.rem(row, 2)

    def other_layer(d):
        return lax.rem(layer + d, layers)

    def other_row(d):
        return lax.rem(row + d, rows)

    def to(l, r):
        return {"layer": l, "row": r}

    def send(src, dst, send_sem, recv_sem, device):
        return pltpu.make_async_remote_copy(
            src_ref=src, dst_ref=dst, send_sem=send_sem, recv_sem=recv_sem,
            device_id=device, device_id_type=pl.DeviceIdType.MESH,
        )

    def here(dst, sem):
        send(dst, dst, sem, sem, to(layer, sibling)).wait_recv()

    def sent(src, sem):
        send(src, src, sem, sem, to(layer, sibling)).wait_send()

    def pl_piece(l, r):
        return plw.at[l, :, pl.ds(pl.multiple_of(r * piece, piece), piece)]

    def pr_piece(r):
        return prw.at[:, pl.ds(pl.multiple_of(r * piece, piece), piece)]

    def p_strip(l, r):
        used = (l + 1) * rows * strip
        used = min(width, -(-used // 128) * 128)
        start = pl.multiple_of((l * rows + r) * strip, strip)
        return pw.at[pl.ds(start, strip), pl.ds(0, used)]

    barrier = pltpu.get_barrier_semaphore()
    for d in range(1, layers):
        pl.semaphore_signal(
            barrier, inc=1, device_id=to(other_layer(d), row), device_id_type=pl.DeviceIdType.MESH
        )
    for d in range(1, rows):
        pl.semaphore_signal(
            barrier, inc=1, device_id=to(layer, other_row(d)), device_id_type=pl.DeviceIdType.MESH
        )
    mine = pl.ds(pl.multiple_of(row * piece, piece), piece)
    prw[:, mine] = pr_ref[...]
    plw[layer, :, mine] = pl_ref[...]
    own_rows = pl.ds(pl.multiple_of((layer * rows + row) * strip, strip), strip)
    pw[own_rows, :] = pf_ref[...]
    pl.semaphore_wait(barrier, layers + rows - 2)

    for d in range(1, rows):
        send(pr_piece(row), pr_piece(row), pr_send.at[d], pr_recv.at[row], to(layer, other_row(d))).start()
        send(
            pl_piece(layer, row), pl_piece(layer, row), pl_send.at[d], pl_recv.at[layer, row],
            to(layer, other_row(d)),
        ).start()
    for d in range(1, layers):
        send(
            pl_piece(layer, row), pl_piece(layer, row), plz_send.at[d], pl_recv.at[layer, row],
            to(other_layer(d), row),
        ).start()
    for l in range(layers):

        @pl.when(layer == l)
        def _():
            for d in range(1, layers):
                send(
                    p_strip(l, row), p_strip(l, row), pz_send.at[d], p_recv.at[l, row],
                    to(other_layer(d), row),
                ).start()
            for d in range(1, chips):
                send(
                    p_strip(l, row), p_strip(l, row), pf_send.at[l, d], p_recv.at[l, row],
                    to(layer, other_row(2 * d)),
                ).start()

    for l in range(layers):
        for s in range(count[l]):
            t = first[l] + s

            @pl.when(layer != l)
            def _():
                send(
                    tl_ref.at[t], zbuf.at[s, layer + 1], tl_send.at[t], tl_recv.at[s, layer], to(l, row)
                ).start()

            @pl.when(layer == l)
            def _():
                zbuf[s, layer + 1] = tl_ref[t]

    fbuf[...] = jnp.zeros_like(fbuf)
    own_count, own_first = pick(count, layer), pick(first, layer)
    eye = (
        lax.broadcasted_iota(jnp.int32, (rank, rank), 0) == lax.broadcasted_iota(jnp.int32, (rank, rank), 1)
    ).astype(F32)
    for s in range(slots):
        t = own_first + jnp.minimum(s, own_count - 1)
        zbuf[s, 0] = ol_ref[t]
        fbuf[s, 0:rank, 0:rank] = dot(or_ref[t], sk_ref[...], NT)
        fbuf[s, 0:rank, rank : 2 * rank] = eye

    for d in range(1, rows):
        here(pr_piece(other_row(d)), pr_recv.at[other_row(d)])
        here(pl_piece(layer, other_row(d)), pl_recv.at[layer, other_row(d)])
    coupling = dot(tr_ref[...].reshape(tiles * rank, width), prw[...], NT)
    sketched = dot(plw[layer], sk_ref[...], NT)
    chained = dot(coupling, sketched, NN, HIGHEST)
    for t in range(tiles):
        weight = -(mask_ref[t, 0].astype(F32))
        block = slice(t * rank, (t + 1) * rank)
        ce[t, :, 0:rank] = chained[block] * weight
        ce[t, :, rank : 2 * rank] = coupling[block] * weight
    for l in range(layers):
        for s in range(count[l]):
            t = first[l] + s

            @pl.when(layer != l)
            def _():
                send(
                    ce.at[t], cebuf.at[s, layer], ce_send.at[t], ce_recv.at[s, layer], to(l, row)
                ).start()

            @pl.when(layer == l)
            def _():
                cebuf[s, layer] = ce[t]

    for l in range(layers):

        @pl.when(layer != l)
        def _():
            here(pl_piece(l, row), pl_recv.at[l, row])
            for d in range(1, rows):
                send(
                    pl_piece(l, row), pl_piece(l, row), plf_send.at[l, d], pl_recv.at[l, row],
                    to(layer, other_row(d)),
                ).start()
            here(p_strip(l, row), p_recv.at[l, row])
            for d in range(1, chips):
                send(
                    p_strip(l, row), p_strip(l, row), pf_send.at[l, d], p_recv.at[l, row],
                    to(layer, other_row(2 * d)),
                ).start()

    for d in range(chips):
        for l in range(layers):
            r = other_row(2 * d)
            if d:
                here(p_strip(l, r), p_recv.at[l, r])
            send(
                p_strip(l, r), p_strip(l, r), p3_send.at[l, d], p_recv.at[l, r], to(layer, sibling)
            ).start()

    for l in range(layers):

        @pl.when(layer == l)
        def _():
            for s in range(count[l]):
                for k in range(layers):
                    if k != l:
                        here(zbuf.at[s, k + 1], tl_recv.at[s, k])
                        here(cebuf.at[s, k], ce_recv.at[s, k])

    parts = []
    for s in range(slots):
        at = jnp.minimum(s, own_count - 1)
        z = zbuf[at].reshape((layers + 1) * rank, width)
        gram = dot(z, z, NT)
        for k in range(layers):
            block = slice((k + 1) * rank, (k + 2) * rank)
            fbuf[s, block, 0:rank] = cebuf[at, k, :, 0:rank]
            fbuf[s, block, (k + 2) * rank : (k + 3) * rank] = cebuf[at, k, :, rank : 2 * rank]
        joined = dot(fbuf[s, :, 0:rank], gram, TN, HIGHEST)
        parts.append(dot(joined, fbuf[s], NN, HIGHEST)[None])
    found = eliminate(jnp.concatenate(parts, axis=0), rank)
    for l in range(layers):

        @pl.when(layer == l)
        def _():
            for s in range(count[l]):
                t = first[l] + s
                mall[t] = found[s]
                for d in range(1, layers):
                    send(
                        mall.at[t], mall.at[t], m_send.at[t, d], m_recv.at[t], to(other_layer(d), row)
                    ).start()

    for l in range(layers):
        for d in range(chips):
            r = lax.rem(sibling + 2 * d, rows)
            here(p_strip(l, r), p_recv.at[l, r])
    chunk = 256
    half = chunk // 2
    for c in range(width // chunk):
        lo, mid, hi = c * chunk, c * chunk + half, (c + 1) * chunk
        top = invert_lower(pw[lo:mid, lo:mid], half, half)
        bottom = invert_lower(pw[mid:hi, mid:hi], half, half)
        cross = dot(bottom, dot(pw[mid:hi, lo:mid], top, NN, HIGHEST), NN, HIGHEST)
        diag[c, 0:half, 0:half] = top
        diag[c, 0:half, half:chunk] = jnp.zeros_like(top)
        diag[c, half:chunk, 0:half] = -cross
        diag[c, half:chunk, half:chunk] = bottom

    for l in range(layers):

        @pl.when(layer != l)
        def _():
            for d in range(1, rows):
                here(pl_piece(l, other_row(d)), pl_recv.at[l, other_row(d)])
            for s in range(count[l]):
                here(mall.at[first[l] + s], m_recv.at[first[l] + s])

    panels = plw[...].reshape(layers * rank, width)
    for t in range(tiles):
        high, low = split(mall[t, :, rank : 2 * rank])
        core[t * rank : (t + 1) * rank, :] = dot(high, or_ref[t], NN) + dot(low, or_ref[t], NN)
    high, low = split(mall[:, :, 2 * rank :].reshape(tiles * rank, layers * rank))
    solved = []
    for c in range(width // chunk):
        cols = slice(c * chunk, (c + 1) * chunk)
        rest = core[:, cols] + (dot(high, panels[:, cols], NN) + dot(low, panels[:, cols], NN))
        for i in range(c):
            rest = rest - dot3(solved[i], split(pw[cols, i * chunk : (i + 1) * chunk]), NT)
        x = dot3(split(rest), split(diag[c]), NT)
        out_ref[:, :, cols] = x.reshape(tiles, rank, chunk)
        solved.append(split(x))

    for d in range(1, rows):
        sent(pr_piece(row), pr_send.at[d])
        sent(pl_piece(layer, row), pl_send.at[d])
    for d in range(1, layers):
        sent(pl_piece(layer, row), plz_send.at[d])
    for l in range(layers):
        for d in range(1, chips):
            sent(p_strip(l, row), pf_send.at[l, d])
        for d in range(chips):
            sent(p_strip(l, other_row(2 * d)), p3_send.at[l, d])

        @pl.when(layer == l)
        def _():
            for d in range(1, layers):
                sent(p_strip(l, row), pz_send.at[d])
                for s in range(count[l]):
                    sent(mall.at[first[l] + s], m_send.at[first[l] + s, d])

        @pl.when(layer != l)
        def _():
            for d in range(1, rows):
                sent(pl_piece(l, row), plf_send.at[l, d])
            for s in range(count[l]):
                sent(tl_ref.at[first[l] + s], tl_send.at[first[l] + s])
                sent(ce.at[first[l] + s], ce_send.at[first[l] + s])


def shards_kernel(layers, rows, tile_left, tile_right, tile_mask, orig_left, orig_right, pivot_left, pivot_right, sketch, pivot_factor):
    tiles, _, rank, width = tile_left.shape
    slots = max(owners(tiles, layers)[0])
    dma = pltpu.SemaphoreType.DMA
    vmem = pl.BlockSpec(memory_space=pltpu.VMEM)
    lanes = (layers + 2) * rank
    return pl.pallas_call(
        partial(kernel, layers, rows),
        out_shape=jax.ShapeDtypeStruct((tiles, rank, width), F32),
        in_specs=[pl.BlockSpec(memory_space=pltpu.SMEM)] + [vmem] * 8,
        out_specs=vmem,
        scratch_shapes=[
            pltpu.VMEM((rank, width), BF16),
            pltpu.VMEM((layers, rank, width), BF16),
            pltpu.VMEM((width, width), F32),
            pltpu.VMEM((slots, layers + 1, rank, width), BF16),
            pltpu.VMEM((tiles, rank, 2 * rank), F32),
            pltpu.VMEM((slots, layers, rank, 2 * rank), F32),
            pltpu.VMEM((slots, (layers + 1) * rank, lanes), F32),
            pltpu.VMEM((tiles, rank, lanes), F32),
            pltpu.VMEM((width // 256, 256, 256), F32),
            pltpu.VMEM((tiles * rank, width), F32),
            dma((rows,)), dma((rows,)), dma((rows,)), dma((layers, rows)),
            dma((layers,)), dma((layers, rows)), dma((layers, rows)), dma((layers, rows)),
            dma((layers,)), dma((layers, rows)),
            dma((tiles,)), dma((slots, layers)), dma((tiles,)), dma((slots, layers)),
            dma((tiles, layers)), dma((tiles,)),
        ],
        compiler_params=pltpu.CompilerParams(
            collective_id=0, has_side_effects=True, vmem_limit_bytes=50 * 1024 * 1024
        ),
    )(
        tile_mask, tile_left.reshape(tiles, rank, width), tile_right.reshape(tiles, rank, width),
        orig_left, orig_right, pivot_left.reshape(rank, -1), pivot_right.reshape(rank, -1),
        sketch, pivot_factor,
    )


def shards_general(
    tile_left,
    tile_right,
    tile_mask,
    orig_left,
    orig_right,
    pivot_left,
    pivot_right,
    sketch,
    pivot_factor,
):
    highest = HIGHEST
    pivot_whole = lax.all_gather(pivot_factor, ("layer", "row"), axis=0, tiled=True)
    left_whole, right_whole = (
        lax.all_gather(pivot_left, "row", axis=2, tiled=True),
        lax.all_gather(pivot_right, "row", axis=2, tiled=True),
    )
    coupling = jnp.einsum("tpqb,psb->tpqs", tile_right, right_whole, preferred_element_type=F32)
    weights = tile_mask.astype(F32)[:, :, None, None]
    update_left = jnp.einsum("tpqs,tpqb->tpsb", coupling, tile_left.astype(F32), precision=highest) * weights
    sketched = jnp.einsum("pqb,sb->pqs", left_whole, sketch, preferred_element_type=F32)
    partial_sample = jnp.einsum("tpqb,pqs->tsb", update_left, sketched, precision=highest)
    orig_float = orig_left.astype(F32)
    orig_sketch = jnp.einsum("tqb,sb->tqs", orig_right, sketch, preferred_element_type=F32)
    own_sample = jnp.einsum("tqb,tqs->tsb", orig_float, orig_sketch, precision=highest)
    sample = own_sample - lax.psum(partial_sample, "layer")
    gram_matrix = jnp.einsum("tqb,tsb->tqs", sample, sample, precision=highest)
    factor = jnp.linalg.cholesky(gram_matrix)
    row_basis = jax.vmap(partial(jax.scipy.linalg.solve_triangular, lower=True))(factor, sample)
    projected = jnp.einsum("tpqb,tsb->tpqs", update_left, row_basis, precision=highest)
    partial_core = jnp.einsum("pqb,tpqs->tsb", left_whole.astype(F32), projected, precision=highest)
    orig_basis = jnp.einsum("tqb,tsb->tqs", orig_float, row_basis, precision=highest)
    own_core = jnp.einsum("tqb,tqs->tsb", orig_right.astype(F32), orig_basis, precision=highest)
    core = own_core - lax.psum(partial_core, "layer")
    tile_count, rank_rows, cell_count = core.shape
    right_sides = core.reshape(tile_count * rank_rows, cell_count).T
    solution = jax.scipy.linalg.solve_triangular(pivot_whole, right_sides, lower=True)
    return solution.T.reshape(tile_count, rank_rows, cell_count)


def solution(mesh):
    in_specs = (
        P("row", "layer", None, None),
        P("row", "layer", None, None),
        P("row", "layer"),
        P("row", None, None),
        P("row", None, None),
        P("layer", None, "row"),
        P("layer", None, "row"),
        P(),
        P(("layer", "row"), None),
    )
    out_specs = P("row", None, None)
    layers, rows = mesh.shape["layer"], mesh.shape["row"]

    def shards(*blocks):
        tiles, panels, rank, width = blocks[0].shape
        fits = (
            panels == 1 and tiles >= layers and rank == 64 and width % 256 == 0 and rows % 2 == 0
            and width % (128 * rows) == 0 and width % (8 * layers * rows) == 0
        )
        if fits:
            return shards_kernel(layers, rows, *blocks)
        return shards_general(*blocks)

    return jax.shard_map(shards, mesh=mesh, in_specs=in_specs, out_specs=out_specs, check_vma=False)
```

time: 419 us -> 89.4 us (0.21)
  the two profiles are of different devices: /device:TPU:1 before, /device:TPU:0 now
where the time goes in v1:
time: 89.4 us; the launch traced here: 88.9 us
  Pallas kernels  77.6 us (87%)
  local copies, waits for them, and re-layouts  11.2 us (13%)
    pallas_call x1, Pallas kernels, shards_kernel(): pl.pallas_call(partial(kernel, layers, rows), out_shape=jax.ShapeDtypeStr...  77.6 us
    unnamed x18, local copies, waits for them, and re-layouts  11.2 us

profile of v1, /device:TPU:0, one launch (start us, length us, event | category | flops | bytes accessed | tf_op | source)
XLA Modules:
  0.0 88.9 jit_solution(12112253739910539630)
XLA Ops:
  0.0 0.7 copy.10.mask_ref
  0.7 0.0 copy-start
  0.7 1.1 %copy-done = bf16[6,1,64,1024]{3,2,1,0:T(8,128)(2,1)S(1)} copy-done((bf16[6,1,64,1024]{3,2,1,0:T(8,128)(2,1)S(1)}, bf16[6,1,64,1024]{3,2,1,0:T(8,128)(2,1)}, u32[]{:S(2)}) %copy-start) | copy-done | bytes 786456
  1.9 0.0 copy-start.1
  1.9 1.1 %copy-done.1 = bf16[6,1,64,1024]{3,2,1,0:T(8,128)(2,1)S(1)} copy-done((bf16[6,1,64,1024]{3,2,1,0:T(8,128)(2,1)S(1)}, bf16[6,1,64,1024]{3,2,1,0:T(8,128)(2,1)}, u32[]{:S(2)}) %copy-start.1) | copy-done | bytes 786456
  3.0 0.0 copy-start.2
  3.0 1.1 %copy-done.2 = bf16[6,64,1024]{2,1,0:T(8,128)(2,1)S(1)} copy-done((bf16[6,64,1024]{2,1,0:T(8,128)(2,1)S(1)}, bf16[6,64,1024]{2,1,0:T(8,128)(2,1)}, u32[]{:S(2)}) %copy-start.2) | copy-done | bytes 786456
  4.1 0.0 copy-start.3
  4.1 1.1 %copy-done.3 = bf16[6,64,1024]{2,1,0:T(8,128)(2,1)S(1)} copy-done((bf16[6,64,1024]{2,1,0:T(8,128)(2,1)S(1)}, bf16[6,64,1024]{2,1,0:T(8,128)(2,1)}, u32[]{:S(2)}) %copy-start.3) | copy-done | bytes 786456
  5.3 0.0 copy-start.4
  5.3 0.9 %copy-done.4 = bf16[64,1024]{1,0:T(8,128)(2,1)S(1)} copy-done((bf16[64,1024]{1,0:T(8,128)(2,1)S(1)}, bf16[64,1024]{1,0:T(8,128)(2,1)}, u32[]{:S(2)}) %copy-start.4) | copy-done | bytes 131096
  6.2 0.0 copy-start.5
  6.2 0.9 %copy-done.5 = f32[32,1024]{1,0:T(8,128)S(1)} copy-done((f32[32,1024]{1,0:T(8,128)S(1)}, f32[32,1024]{1,0:T(8,128)}, u32[]{:S(2)}) %copy-start.5) | copy-done | bytes 131096
  7.1 0.0 copy-start.6
  7.1 0.7 copy-done.6
  7.8 0.0 copy-start.7
  7.8 0.7 copy-done.7
  8.5 77.6 %shard_map.91 = f32[6,64,1024]{2,1,0:T(8,128)} custom-call(s32[6,1]{1,0:T(8,128)S(1)} %copy.10.mask_ref, bf16[6,64,1024]{2,1,0:T(8,128)(2,1)S(1)} %bitcast.4, bf16[6,64,1024]{2,1,0:T(8,128)(2,1)S(1)} %bitcast.5, bf16[6,64,1024]{2,1,0:T(8,128)(2,1)S(1)} %copy-done.2, bf16[6,64,1024]{2,1,0:T(8,128)(2,1)S(1)} %copy-done.3, bf16[64,128]{1,0:T(8,128)(2,1)S(1)} %bitcast.6, ...), custom_call_target="tpu_custom_call" | custom-call | tf_op jit(solution)/shard_map/pallas_call | solution.py:355
  86.2 2.7 %copy.12 = f32[6,64,1024]{2,1,0:T(8,128)} copy(f32[6,64,1024]{2,1,0:T(8,128)} %shard_map.91) | data formatting | bytes 3145728
Async XLA Ops:
  0.7 1.1 %copy-start = (bf16[6,1,64,1024]{3,2,1,0:T(8,128)(2,1)S(1)}, bf16[6,1,64,1024]{3,2,1,0:T(8,128)(2,1)}, u32[]{:S(2)}) copy-start(bf16[6,1,64,1024]{3,2,1,0:T(8,128)(2,1)} %param.9) | copy-start | bytes 2359300
  1.9 1.1 %copy-start.1 = (bf16[6,1,64,1024]{3,2,1,0:T(8,128)(2,1)S(1)}, bf16[6,1,64,1024]{3,2,1,0:T(8,128)(2,1)}, u32[]{:S(2)}) copy-start(bf16[6,1,64,1024]{3,2,1,0:T(8,128)(2,1)} %param.10) | copy-start | bytes 2359300
  3.0 1.1 %copy-start.2 = (bf16[6,64,1024]{2,1,0:T(8,128)(2,1)S(1)}, bf16[6,64,1024]{2,1,0:T(8,128)(2,1)}, u32[]{:S(2)}) copy-start(bf16[6,64,1024]{2,1,0:T(8,128)(2,1)} %ol_ref.1) | copy-start | bytes 2359300
  4.1 1.1 %copy-start.3 = (bf16[6,64,1024]{2,1,0:T(8,128)(2,1)S(1)}, bf16[6,64,1024]{2,1,0:T(8,128)(2,1)}, u32[]{:S(2)}) copy-start(bf16[6,64,1024]{2,1,0:T(8,128)(2,1)} %or_ref.1) | copy-start | bytes 2359300
  5.3 0.9 %copy-start.4 = (bf16[64,1024]{1,0:T(8,128)(2,1)S(1)}, bf16[64,1024]{1,0:T(8,128)(2,1)}, u32[]{:S(2)}) copy-start(bf16[64,1024]{1,0:T(8,128)(2,1)} %sk_ref.1) | copy-start | bytes 393220
  6.2 0.9 %copy-start.5 = (f32[32,1024]{1,0:T(8,128)S(1)}, f32[32,1024]{1,0:T(8,128)}, u32[]{:S(2)}) copy-start(f32[32,1024]{1,0:T(8,128)} %pf_ref.1) | copy-start | bytes 393220
  7.1 0.7 copy-start.6
  7.8 0.7 copy-start.7

commit v2 on v1

--- a/solution.py
+++ b/solution.py
@@ -44,46 +44,54 @@
     return value
 
 
-def invert_lower(block, size, stop):
+def invert_lower(blocks, size):
     rows = lax.broadcasted_iota(jnp.int32, (size, size), 0)
     cols = lax.broadcasted_iota(jnp.int32, (size, size), 1)
     eye = rows == cols
-    inverse = jnp.where(eye, 1.0 / jnp.where(eye, block, 1.0), 0.0)
+    inverses = [jnp.where(eye, 1.0 / jnp.where(eye, block, 1.0), 0.0) for block in blocks]
     step = 1
-    while step < stop:
+    while step < size:
         pair = (rows // (2 * step) == cols // (2 * step)) & (rows // step > cols // step)
-        below = jnp.where(pair, block, 0.0)
-        inverse = inverse - dot(inverse, dot(below, inverse, NN, HIGHEST), NN, HIGHEST)
+        inner = [
+            dot(jnp.where(pair, block, 0.0), inverse, NN, HIGHEST) for block, inverse in zip(blocks, inverses)
+        ]
+        outer = [dot(inverse, right, NN, HIGHEST) for inverse, right in zip(inverses, inner)]
+        inverses = [inverse - change for inverse, change in zip(inverses, outer)]
         step *= 2
-    return inverse
+    return inverses
 
 
 def eliminate(augmented, rank):
-    done = []
-    left = augmented
+    lanes = 128
+    tiles = [augmented[:, :, i : i + lanes] for i in range(0, augmented.shape[2], lanes)]
+    done = [[] for _ in tiles]
+    roots = []
     for block in range(rank // 8):
-        index = lax.broadcasted_iota(jnp.int32, (left.shape[0], left.shape[1], 1), 1)
+        shape = tiles[0].shape
+        index = lax.broadcasted_iota(jnp.int32, shape, 1)
+        columns = [
+            jnp.broadcast_to(tiles[0][:, :, block * 8 + at : block * 8 + at + 1], shape) for at in range(8)
+        ]
         for at in range(8):
-            column = block * 8 + at
-            pivot = left[:, at : at + 1, :]
-            scale = 1.0 / pivot[:, :, column : column + 1]
-            weight = jnp.where(index > at, left[:, :, column : column + 1] * scale, 0.0)
-            left = left - weight * pivot
-        done.append(left[:, :8, :])
-        left = left[:, 8:, :]
-    whole = jnp.concatenate(done, axis=1)
-    lanes = lax.broadcasted_iota(jnp.int32, whole.shape, 2)
-    index = lax.broadcasted_iota(jnp.int32, whole.shape, 1)
-    diagonal = jnp.sum(jnp.where(lanes == index, whole, 0.0), axis=2, keepdims=True)
-    return whole * lax.rsqrt(diagonal)
+            pivot = columns[at][:, at : at + 1, :]
+            weight = jnp.where(index > at, columns[at] * (1.0 / pivot), 0.0)
+            for later in range(at + 1, 8):
+                columns[later] = columns[later] - weight * columns[later][:, at : at + 1, :]
+            tiles = [tile - weight * tile[:, at : at + 1, :] for tile in tiles]
+            roots.append(lax.rsqrt(pivot))
+        for i, tile in enumerate(tiles):
+            done[i].append(tile[:, :8, :])
+        tiles = [tile[:, 8:, :] for tile in tiles]
+    scale = jnp.concatenate(roots, axis=1)
+    return jnp.concatenate([jnp.concatenate(part, axis=1) * scale for part in done], axis=2)
 
 
 def kernel(
     layers, rows, mask_ref, tl_ref, tr_ref, ol_ref, or_ref, pl_ref, pr_ref, sk_ref, pf_ref,
     out_ref,
-    prw, plw, pw, zbuf, ce, cebuf, fbuf, mall, diag, core,
+    prw, plw, pw, zbuf, ce, cebuf, fbuf, mall, diag, below, core, trv, orv, skv, xv,
     pr_send, pr_recv, pl_send, pl_recv, pz_send, pf_send, p3_send, p_recv,
-    plz_send, plf_send, tl_send, tl_recv, ce_send, ce_recv, m_send, m_recv,
+    plz_send, plf_send, tl_send, tl_recv, ce_send, ce_recv, m_send, m_recv, load, local, leave,
 ):
     layer, row = lax.axis_index("layer"), lax.axis_index("row")
     tiles, rank, width = tl_ref.shape
@@ -121,11 +129,15 @@
     def pr_piece(r):
         return prw.at[:, pl.ds(pl.multiple_of(r * piece, piece), piece)]
 
+    def used(l):
+        return min(width, -(-((l + 1) * rows * strip) // 128) * 128)
+
     def p_strip(l, r):
-        used = (l + 1) * rows * strip
-        used = min(width, -(-used // 128) * 128)
         start = pl.multiple_of((l * rows + r) * strip, strip)
-        return pw.at[pl.ds(start, strip), pl.ds(0, used)]
+        return pw.at[pl.ds(start, strip), pl.ds(0, used(l))]
+
+    def own_strip(l):
+        return pf_ref.at[:, pl.ds(0, used(l))]
 
     barrier = pltpu.get_barrier_semaphore()
     for d in range(1, layers):
@@ -136,22 +148,32 @@
         pl.semaphore_signal(
             barrier, inc=1, device_id=to(layer, other_row(d)), device_id_type=pl.DeviceIdType.MESH
         )
-    mine = pl.ds(pl.multiple_of(row * piece, piece), piece)
-    prw[:, mine] = pr_ref[...]
-    plw[layer, :, mine] = pl_ref[...]
+    own_count, own_first = pick(count, layer), pick(first, layer)
     own_rows = pl.ds(pl.multiple_of((layer * rows + row) * strip, strip), strip)
-    pw[own_rows, :] = pf_ref[...]
+    loads = [
+        pltpu.make_async_copy(src, dst, load.at[i])
+        for i, (src, dst) in enumerate([
+            (pr_ref, pr_piece(row)), (pl_ref, pl_piece(layer, row)), (sk_ref, skv), (tr_ref, trv),
+            (or_ref, orv), (pf_ref, pw.at[own_rows, :]),
+        ])
+    ]
+    for s in range(slots):
+        t = own_first + jnp.minimum(s, own_count - 1)
+        loads.append(pltpu.make_async_copy(ol_ref.at[t], zbuf.at[s, 0], local.at[0, s]))
+        loads.append(pltpu.make_async_copy(tl_ref.at[t], zbuf.at[s, layer + 1], local.at[1, s]))
+    for copy in loads:
+        copy.start()
     pl.semaphore_wait(barrier, layers + rows - 2)
 
     for d in range(1, rows):
-        send(pr_piece(row), pr_piece(row), pr_send.at[d], pr_recv.at[row], to(layer, other_row(d))).start()
+        send(pr_ref, pr_piece(row), pr_send.at[d], pr_recv.at[row], to(layer, other_row(d))).start()
         send(
-            pl_piece(layer, row), pl_piece(layer, row), pl_send.at[d], pl_recv.at[layer, row],
+            pl_ref, pl_piece(layer, row), pl_send.at[d], pl_recv.at[layer, row],
             to(layer, other_row(d)),
         ).start()
     for d in range(1, layers):
         send(
-            pl_piece(layer, row), pl_piece(layer, row), plz_send.at[d], pl_recv.at[layer, row],
+            pl_ref, pl_piece(layer, row), plz_send.at[d], pl_recv.at[layer, row],
             to(other_layer(d), row),
         ).start()
     for l in range(layers):
@@ -160,12 +182,12 @@
         def _():
             for d in range(1, layers):
                 send(
-                    p_strip(l, row), p_strip(l, row), pz_send.at[d], p_recv.at[l, row],
+                    own_strip(l), p_strip(l, row), pz_send.at[d], p_recv.at[l, row],
                     to(other_layer(d), row),
                 ).start()
             for d in range(1, chips):
                 send(
-                    p_strip(l, row), p_strip(l, row), pf_send.at[l, d], p_recv.at[l, row],
+                    own_strip(l), p_strip(l, row), pf_send.at[l, d], p_recv.at[l, row],
                     to(layer, other_row(2 * d)),
                 ).start()
 
@@ -179,26 +201,22 @@
                     tl_ref.at[t], zbuf.at[s, layer + 1], tl_send.at[t], tl_recv.at[s, layer], to(l, row)
                 ).start()
 
-            @pl.when(layer == l)
-            def _():
-                zbuf[s, layer + 1] = tl_ref[t]
-
     fbuf[...] = jnp.zeros_like(fbuf)
-    own_count, own_first = pick(count, layer), pick(first, layer)
     eye = (
         lax.broadcasted_iota(jnp.int32, (rank, rank), 0) == lax.broadcasted_iota(jnp.int32, (rank, rank), 1)
     ).astype(F32)
+    for copy in loads:
+        copy.wait()
     for s in range(slots):
         t = own_first + jnp.minimum(s, own_count - 1)
-        zbuf[s, 0] = ol_ref[t]
-        fbuf[s, 0:rank, 0:rank] = dot(or_ref[t], sk_ref[...], NT)
+        fbuf[s, 0:rank, 0:rank] = dot(orv[t], skv[...], NT)
         fbuf[s, 0:rank, rank : 2 * rank] = eye
 
     for d in range(1, rows):
         here(pr_piece(other_row(d)), pr_recv.at[other_row(d)])
         here(pl_piece(layer, other_row(d)), pl_recv.at[layer, other_row(d)])
-    coupling = dot(tr_ref[...].reshape(tiles * rank, width), prw[...], NT)
-    sketched = dot(plw[layer], sk_ref[...], NT)
+    coupling = dot(trv[...].reshape(tiles * rank, width), prw[...], NT)
+    sketched = dot(plw[layer], skv[...], NT)
     chained = dot(coupling, sketched, NN, HIGHEST)
     for t in range(tiles):
         weight = -(mask_ref[t, 0].astype(F32))
@@ -273,7 +291,11 @@
         def _():
             for s in range(count[l]):
                 t = first[l] + s
-                mall[t] = found[s]
+                high, low = split(found[s][:, rank:])
+                mall[t, :, 0:rank] = high[:, 0:rank]
+                mall[t, :, rank : 2 * rank] = low[:, 0:rank]
+                mall[t, :, 2 * rank : (layers + 2) * rank] = high[:, rank:]
+                mall[t, :, (layers + 2) * rank :] = low[:, rank:]
                 for d in range(1, layers):
                     send(
                         mall.at[t], mall.at[t], m_send.at[t, d], m_recv.at[t], to(other_layer(d), row)
@@ -285,15 +307,27 @@
             here(p_strip(l, r), p_recv.at[l, r])
     chunk = 256
     half = chunk // 2
-    for c in range(width // chunk):
-        lo, mid, hi = c * chunk, c * chunk + half, (c + 1) * chunk
-        top = invert_lower(pw[lo:mid, lo:mid], half, half)
-        bottom = invert_lower(pw[mid:hi, mid:hi], half, half)
-        cross = dot(bottom, dot(pw[mid:hi, lo:mid], top, NN, HIGHEST), NN, HIGHEST)
-        diag[c, 0:half, 0:half] = top
-        diag[c, 0:half, half:chunk] = jnp.zeros_like(top)
-        diag[c, half:chunk, 0:half] = -cross
-        diag[c, half:chunk, half:chunk] = bottom
+    chunks = width // chunk
+    inverses = invert_lower(
+        [pw[i * half : (i + 1) * half, i * half : (i + 1) * half] for i in range(2 * chunks)], half
+    )
+    inner = [
+        dot(pw[c * chunk + half : (c + 1) * chunk, c * chunk : c * chunk + half], inverses[2 * c], NN, HIGHEST)
+        for c in range(chunks)
+    ]
+    for c in range(chunks):
+        cross = dot(inverses[2 * c + 1], inner[c], NN, HIGHEST)
+        for part, value in enumerate(split(inverses[2 * c])):
+            diag[part, c, 0:half, 0:half] = value
+        for part, value in enumerate(split(inverses[2 * c + 1])):
+            diag[part, c, half:chunk, half:chunk] = value
+        for part, value in enumerate(split(-cross)):
+            diag[part, c, half:chunk, 0:half] = value
+            diag[part, c, 0:half, half:chunk] = jnp.zeros_like(value)
+        if c:
+            rows_at = slice(c * chunk, (c + 1) * chunk)
+            for part, value in enumerate(split(pw[rows_at, 0 : c * chunk])):
+                below[part, rows_at, 0 : c * chunk] = value
 
     for l in range(layers):
 
@@ -306,19 +340,32 @@
 
     panels = plw[...].reshape(layers * rank, width)
     for t in range(tiles):
-        high, low = split(mall[t, :, rank : 2 * rank])
-        core[t * rank : (t + 1) * rank, :] = dot(high, or_ref[t], NN) + dot(low, or_ref[t], NN)
-    high, low = split(mall[:, :, 2 * rank :].reshape(tiles * rank, layers * rank))
+        core[t * rank : (t + 1) * rank, :] = dot(mall[t, :, 0:rank], orv[t], NN) + dot(
+            mall[t, :, rank : 2 * rank], orv[t], NN
+        )
+    high = mall[:, :, 2 * rank : (layers + 2) * rank].reshape(tiles * rank, layers * rank)
+    low = mall[:, :, (layers + 2) * rank :].reshape(tiles * rank, layers * rank)
     solved = []
-    for c in range(width // chunk):
+    outs = []
+    for c in range(chunks):
         cols = slice(c * chunk, (c + 1) * chunk)
         rest = core[:, cols] + (dot(high, panels[:, cols], NN) + dot(low, panels[:, cols], NN))
         for i in range(c):
-            rest = rest - dot3(solved[i], split(pw[cols, i * chunk : (i + 1) * chunk]), NT)
-        x = dot3(split(rest), split(diag[c]), NT)
-        out_ref[:, :, cols] = x.reshape(tiles, rank, chunk)
-        solved.append(split(x))
-
+            at = slice(i * chunk, (i + 1) * chunk)
+            rest = rest - dot3(solved[i], (below[0, cols, at], below[1, cols, at]), NT)
+        x = dot3(split(rest), (diag[0, c], diag[1, c]), NT)
+        xv[:, :, cols] = x.reshape(tiles, rank, chunk)
+        outs.append(
+            pltpu.make_async_copy(
+                xv.at[:, :, pl.ds(c * chunk, chunk)], out_ref.at[:, :, pl.ds(c * chunk, chunk)], leave.at[c]
+            )
+        )
+        outs[-1].start()
+        if c + 1 < chunks:
+            solved.append(split(x))
+
+    for copy in outs:
+        copy.wait()
     for d in range(1, rows):
         sent(pr_piece(row), pr_send.at[d])
         sent(pl_piece(layer, row), pl_send.at[d])
@@ -350,13 +397,13 @@
     tiles, _, rank, width = tile_left.shape
     slots = max(owners(tiles, layers)[0])
     dma = pltpu.SemaphoreType.DMA
-    vmem = pl.BlockSpec(memory_space=pltpu.VMEM)
+    hbm = pl.BlockSpec(memory_space=pl.ANY)
     lanes = (layers + 2) * rank
     return pl.pallas_call(
         partial(kernel, layers, rows),
         out_shape=jax.ShapeDtypeStruct((tiles, rank, width), F32),
-        in_specs=[pl.BlockSpec(memory_space=pltpu.SMEM)] + [vmem] * 8,
-        out_specs=vmem,
+        in_specs=[pl.BlockSpec(memory_space=pltpu.SMEM)] + [hbm] * 8,
+        out_specs=hbm,
         scratch_shapes=[
             pltpu.VMEM((rank, width), BF16),
             pltpu.VMEM((layers, rank, width), BF16),
@@ -365,14 +412,19 @@
             pltpu.VMEM((tiles, rank, 2 * rank), F32),
             pltpu.VMEM((slots, layers, rank, 2 * rank), F32),
             pltpu.VMEM((slots, (layers + 1) * rank, lanes), F32),
-            pltpu.VMEM((tiles, rank, lanes), F32),
-            pltpu.VMEM((width // 256, 256, 256), F32),
+            pltpu.VMEM((tiles, rank, 2 * (layers + 1) * rank), BF16),
+            pltpu.VMEM((2, width // 256, 256, 256), BF16),
+            pltpu.VMEM((2, width, width), BF16),
             pltpu.VMEM((tiles * rank, width), F32),
+            pltpu.VMEM((tiles, rank, width), BF16),
+            pltpu.VMEM((tiles, rank, width), BF16),
+            pltpu.VMEM((rank, width), BF16),
+            pltpu.VMEM((tiles, rank, width), F32),
             dma((rows,)), dma((rows,)), dma((rows,)), dma((layers, rows)),
             dma((layers,)), dma((layers, rows)), dma((layers, rows)), dma((layers, rows)),
             dma((layers,)), dma((layers, rows)),
             dma((tiles,)), dma((slots, layers)), dma((tiles,)), dma((slots, layers)),
-            dma((tiles, layers)), dma((tiles,)),
+            dma((tiles, layers)), dma((tiles,)), dma((6,)), dma((2, slots)), dma((width // 256,)),
         ],
         compiler_params=pltpu.CompilerParams(
             collective_id=0, has_side_effects=True, vmem_limit_bytes=50 * 1024 * 1024

time: 89.4 us -> 72.5 us (0.81)
  the two profiles are of different devices: /device:TPU:0 before, /device:TPU:25 now
where the time goes in v2:
time: 72.5 us; the launch traced here: 72.1 us
  Pallas kernels  60.8 us (84%)
  local copies, waits for them, and re-layouts  11.2 us (15%)
    pallas_call x1, Pallas kernels, shards_kernel(): pl.pallas_call(partial(kernel, layers, rows), out_shape=jax.ShapeDtypeStr...  60.8 us
    unnamed x18, local copies, waits for them, and re-layouts  11.2 us

profile of v2, /device:TPU:25, one launch (start us, length us, event | category | flops | bytes accessed | tf_op | source)
XLA Modules:
  0.0 72.1 jit_solution(15675828549236365245)
XLA Ops:
  0.0 0.7 %copy.10.mask_ref = s32[6,1]{1,0:T(8,128)S(1)} copy(s32[6,1]{0,1:T(1,128)} %param.11) | data formatting | bytes 48 | tf_op args[2]
  0.7 0.0 copy-start
  0.7 1.1 %copy-done = bf16[6,1,64,1024]{3,2,1,0:T(8,128)(2,1)S(1)} copy-done((bf16[6,1,64,1024]{3,2,1,0:T(8,128)(2,1)S(1)}, bf16[6,1,64,1024]{3,2,1,0:T(8,128)(2,1)}, u32[]{:S(2)}) %copy-start) | copy-done | bytes 786456
  1.9 0.0 copy-start.1
  1.9 1.1 %copy-done.1 = bf16[6,1,64,1024]{3,2,1,0:T(8,128)(2,1)S(1)} copy-done((bf16[6,1,64,1024]{3,2,1,0:T(8,128)(2,1)S(1)}, bf16[6,1,64,1024]{3,2,1,0:T(8,128)(2,1)}, u32[]{:S(2)}) %copy-start.1) | copy-done | bytes 786456
  3.0 0.0 copy-start.2
  3.0 1.1 %copy-done.2 = bf16[6,64,1024]{2,1,0:T(8,128)(2,1)S(1)} copy-done((bf16[6,64,1024]{2,1,0:T(8,128)(2,1)S(1)}, bf16[6,64,1024]{2,1,0:T(8,128)(2,1)}, u32[]{:S(2)}) %copy-start.2) | copy-done | bytes 786456
  4.1 0.0 copy-start.3
  4.1 1.1 %copy-done.3 = bf16[6,64,1024]{2,1,0:T(8,128)(2,1)S(1)} copy-done((bf16[6,64,1024]{2,1,0:T(8,128)(2,1)S(1)}, bf16[6,64,1024]{2,1,0:T(8,128)(2,1)}, u32[]{:S(2)}) %copy-start.3) | copy-done | bytes 786456
  5.3 0.0 copy-start.4
  5.3 0.9 %copy-done.4 = bf16[64,1024]{1,0:T(8,128)(2,1)S(1)} copy-done((bf16[64,1024]{1,0:T(8,128)(2,1)S(1)}, bf16[64,1024]{1,0:T(8,128)(2,1)}, u32[]{:S(2)}) %copy-start.4) | copy-done | bytes 131096
  6.2 0.0 copy-start.5
  6.2 0.9 %copy-done.5 = f32[32,1024]{1,0:T(8,128)S(1)} copy-done((f32[32,1024]{1,0:T(8,128)S(1)}, f32[32,1024]{1,0:T(8,128)}, u32[]{:S(2)}) %copy-start.5) | copy-done | bytes 131096
  7.1 0.0 copy-start.6
  7.1 0.7 copy-done.6
  7.8 0.0 copy-start.7
  7.8 0.7 copy-done.7
  8.5 60.8 %shard_map.91 = f32[6,64,1024]{2,1,0:T(8,128)} custom-call(s32[6,1]{1,0:T(8,128)S(1)} %copy.10.mask_ref, bf16[6,64,1024]{2,1,0:T(8,128)(2,1)S(1)} %bitcast.4, bf16[6,64,1024]{2,1,0:T(8,128)(2,1)S(1)} %bitcast.5, bf16[6,64,1024]{2,1,0:T(8,128)(2,1)S(1)} %copy-done.2, bf16[6,64,1024]{2,1,0:T(8,128)(2,1)S(1)} %copy-done.3, bf16[64,128]{1,0:T(8,128)(2,1)S(1)} %bitcast.6, ...), custom_call_target="tpu_custom_call" | custom-call | tf_op jit(solution)/shard_map/pallas_call | solution.py:402
  69.4 2.7 %copy.12 = f32[6,64,1024]{2,1,0:T(8,128)} copy(f32[6,64,1024]{2,1,0:T(8,128)} %shard_map.91) | data formatting | bytes 3145728
Async XLA Ops:
  0.7 1.1 %copy-start = (bf16[6,1,64,1024]{3,2,1,0:T(8,128)(2,1)S(1)}, bf16[6,1,64,1024]{3,2,1,0:T(8,128)(2,1)}, u32[]{:S(2)}) copy-start(bf16[6,1,64,1024]{3,2,1,0:T(8,128)(2,1)} %param.9) | copy-start | bytes 2359300
  1.9 1.1 %copy-start.1 = (bf16[6,1,64,1024]{3,2,1,0:T(8,128)(2,1)S(1)}, bf16[6,1,64,1024]{3,2,1,0:T(8,128)(2,1)}, u32[]{:S(2)}) copy-start(bf16[6,1,64,1024]{3,2,1,0:T(8,128)(2,1)} %param.10) | copy-start | bytes 2359300
  3.0 1.1 %copy-start.2 = (bf16[6,64,1024]{2,1,0:T(8,128)(2,1)S(1)}, bf16[6,64,1024]{2,1,0:T(8,128)(2,1)}, u32[]{:S(2)}) copy-start(bf16[6,64,1024]{2,1,0:T(8,128)(2,1)} %ol_ref.1) | copy-start | bytes 2359300
  4.1 1.1 %copy-start.3 = (bf16[6,64,1024]{2,1,0:T(8,128)(2,1)S(1)}, bf16[6,64,1024]{2,1,0:T(8,128)(2,1)}, u32[]{:S(2)}) copy-start(bf16[6,64,1024]{2,1,0:T(8,128)(2,1)} %or_ref.1) | copy-start | bytes 2359300
  5.3 0.9 %copy-start.4 = (bf16[64,1024]{1,0:T(8,128)(2,1)S(1)}, bf16[64,1024]{1,0:T(8,128)(2,1)}, u32[]{:S(2)}) copy-start(bf16[64,1024]{1,0:T(8,128)(2,1)} %sk_ref.1) | copy-start | bytes 393220
  6.2 0.9 %copy-start.5 = (f32[32,1024]{1,0:T(8,128)S(1)}, f32[32,1024]{1,0:T(8,128)}, u32[]{:S(2)}) copy-start(f32[32,1024]{1,0:T(8,128)} %pf_ref.1) | copy-start | bytes 393220
  7.1 0.7 copy-start.6
  7.8 0.7 copy-start.7

commit v3 on v2

--- a/solution.py
+++ b/solution.py
@@ -12,7 +12,6 @@
 BF16 = jnp.bfloat16
 NN = (((1,), (0,)), ((), ()))
 NT = (((1,), (1,)), ((), ()))
-TN = (((0,), (0,)), ((), ()))
 
 
 def dot(a, b, dims, precision=None):
@@ -27,6 +26,24 @@
 def dot3(a, b, dims):
     (ah, al), (bh, bl) = a, b
     return dot(ah, bh, dims) + (dot(ah, bl, dims) + dot(al, bh, dims))
+
+
+def split3(x):
+    high = x.astype(BF16)
+    rest = x - high.astype(F32)
+    middle = rest.astype(BF16)
+    return high, middle, (rest - middle.astype(F32)).astype(BF16)
+
+
+def dot6(a, b):
+    rows = a.shape[0]
+    stacked = jnp.concatenate(split3(a), axis=0)
+    high, middle, low = split3(b)
+    by_high = dot(stacked, high, NN)
+    by_middle = dot(stacked[: 2 * rows], middle, NN)
+    by_low = dot(stacked[:rows], low, NN)
+    small = by_high[2 * rows :] + by_middle[rows:] + by_low
+    return by_high[:rows] + (by_high[rows : 2 * rows] + by_middle[:rows] + small)
 
 
 def owners(tiles, layers):
@@ -136,6 +153,15 @@
         start = pl.multiple_of((l * rows + r) * strip, strip)
         return pw.at[pl.ds(start, strip), pl.ds(0, used(l))]
 
+    def sides(l, source=None):
+        both = [side for side in (0, 1) if 0 <= l + 2 * side - 1 < layers]
+        if source is None:
+            return both
+        return [side for side in both if side == (source < l)]
+
+    def sources(l):
+        return sorted((i for i in range(layers) if i != l), key=lambda i: (abs(i - l), i))
+
     def own_strip(l):
         return pf_ref.at[:, pl.ds(0, used(l))]
 
@@ -154,7 +180,7 @@
         pltpu.make_async_copy(src, dst, load.at[i])
         for i, (src, dst) in enumerate([
             (pr_ref, pr_piece(row)), (pl_ref, pl_piece(layer, row)), (sk_ref, skv), (tr_ref, trv),
-            (or_ref, orv), (pf_ref, pw.at[own_rows, :]),
+            (or_ref, orv.at[:, 0]), (or_ref, orv.at[:, 1]), (pf_ref, pw.at[own_rows, :]),
         ])
     ]
     for s in range(slots):
@@ -171,19 +197,17 @@
             pl_ref, pl_piece(layer, row), pl_send.at[d], pl_recv.at[layer, row],
             to(layer, other_row(d)),
         ).start()
-    for d in range(1, layers):
-        send(
-            pl_ref, pl_piece(layer, row), plz_send.at[d], pl_recv.at[layer, row],
-            to(other_layer(d), row),
-        ).start()
     for l in range(layers):
 
         @pl.when(layer == l)
         def _():
-            for d in range(1, layers):
+            for side in sides(l):
                 send(
-                    own_strip(l), p_strip(l, row), pz_send.at[d], p_recv.at[l, row],
-                    to(other_layer(d), row),
+                    pl_ref, pl_piece(l, row), plz_send.at[l, side], pl_recv.at[l, row], to(l + 2 * side - 1, row)
+                ).start()
+                send(
+                    own_strip(l), p_strip(l, row), pz_send.at[l, side], p_recv.at[l, row],
+                    to(l + 2 * side - 1, row),
                 ).start()
             for d in range(1, chips):
                 send(
@@ -209,7 +233,7 @@
         copy.wait()
     for s in range(slots):
         t = own_first + jnp.minimum(s, own_count - 1)
-        fbuf[s, 0:rank, 0:rank] = dot(orv[t], skv[...], NT)
+        fbuf[s, 0:rank, 0:rank] = dot(orv[t, 0], skv[...], NT)
         fbuf[s, 0:rank, rank : 2 * rank] = eye
 
     for d in range(1, rows):
@@ -219,7 +243,7 @@
     sketched = dot(plw[layer], skv[...], NT)
     chained = dot(coupling, sketched, NN, HIGHEST)
     for t in range(tiles):
-        weight = -(mask_ref[t, 0].astype(F32))
+        weight = -(mask_ref[t].astype(F32))
         block = slice(t * rank, (t + 1) * rank)
         ce[t, :, 0:rank] = chained[block] * weight
         ce[t, :, rank : 2 * rank] = coupling[block] * weight
@@ -237,31 +261,32 @@
             def _():
                 cebuf[s, layer] = ce[t]
 
-    for l in range(layers):
-
-        @pl.when(layer != l)
-        def _():
-            here(pl_piece(l, row), pl_recv.at[l, row])
-            for d in range(1, rows):
-                send(
-                    pl_piece(l, row), pl_piece(l, row), plf_send.at[l, d], pl_recv.at[l, row],
-                    to(layer, other_row(d)),
-                ).start()
-            here(p_strip(l, row), p_recv.at[l, row])
-            for d in range(1, chips):
-                send(
-                    p_strip(l, row), p_strip(l, row), pf_send.at[l, d], p_recv.at[l, row],
-                    to(layer, other_row(2 * d)),
-                ).start()
-
-    for d in range(chips):
-        for l in range(layers):
-            r = other_row(2 * d)
-            if d:
-                here(p_strip(l, r), p_recv.at[l, r])
-            send(
-                p_strip(l, r), p_strip(l, r), p3_send.at[l, d], p_recv.at[l, r], to(layer, sibling)
-            ).start()
+    for me in range(layers):
+
+        @pl.when(layer == me)
+        def _():
+            for l in sources(me):
+                here(pl_piece(l, row), pl_recv.at[l, row])
+                here(p_strip(l, row), p_recv.at[l, row])
+                for side in sides(me, l):
+                    send(
+                        pl_piece(l, row), pl_piece(l, row), plz_send.at[l, side], pl_recv.at[l, row],
+                        to(me + 2 * side - 1, row),
+                    ).start()
+                    send(
+                        p_strip(l, row), p_strip(l, row), pz_send.at[l, side], p_recv.at[l, row],
+                        to(me + 2 * side - 1, row),
+                    ).start()
+                for d in range(1, rows):
+                    send(
+                        pl_piece(l, row), pl_piece(l, row), plf_send.at[l, d], pl_recv.at[l, row],
+                        to(layer, other_row(d)),
+                    ).start()
+                for d in range(1, chips):
+                    send(
+                        p_strip(l, row), p_strip(l, row), pf_send.at[l, d], p_recv.at[l, row],
+                        to(layer, other_row(2 * d)),
+                    ).start()
 
     for l in range(layers):
 
@@ -282,8 +307,8 @@
             block = slice((k + 1) * rank, (k + 2) * rank)
             fbuf[s, block, 0:rank] = cebuf[at, k, :, 0:rank]
             fbuf[s, block, (k + 2) * rank : (k + 3) * rank] = cebuf[at, k, :, rank : 2 * rank]
-        joined = dot(fbuf[s, :, 0:rank], gram, TN, HIGHEST)
-        parts.append(dot(joined, fbuf[s], NN, HIGHEST)[None])
+        joined = dot6(fbuf[s, :, 0:rank].T, gram)
+        parts.append(dot6(joined, fbuf[s])[None])
     found = eliminate(jnp.concatenate(parts, axis=0), rank)
     for l in range(layers):
 
@@ -300,6 +325,15 @@
                     send(
                         mall.at[t], mall.at[t], m_send.at[t, d], m_recv.at[t], to(other_layer(d), row)
                     ).start()
+
+    for d in range(chips):
+        for l in range(layers):
+            r = other_row(2 * d)
+            if d:
+                here(p_strip(l, r), p_recv.at[l, r])
+            send(
+                p_strip(l, r), p_strip(l, r), p3_send.at[l, d], p_recv.at[l, r], to(layer, sibling)
+            ).start()
 
     for l in range(layers):
         for d in range(chips):
@@ -340,8 +374,8 @@
 
     panels = plw[...].reshape(layers * rank, width)
     for t in range(tiles):
-        core[t * rank : (t + 1) * rank, :] = dot(mall[t, :, 0:rank], orv[t], NN) + dot(
-            mall[t, :, rank : 2 * rank], orv[t], NN
+        core[t * rank : (t + 1) * rank, :] = dot(
+            mall[t, :, 0 : 2 * rank], orv[t].reshape(2 * rank, width), NN
         )
     high = mall[:, :, 2 * rank : (layers + 2) * rank].reshape(tiles * rank, layers * rank)
     low = mall[:, :, (layers + 2) * rank :].reshape(tiles * rank, layers * rank)
@@ -369,8 +403,6 @@
     for d in range(1, rows):
         sent(pr_piece(row), pr_send.at[d])
         sent(pl_piece(layer, row), pl_send.at[d])
-    for d in range(1, layers):
-        sent(pl_piece(layer, row), plz_send.at[d])
     for l in range(layers):
         for d in range(1, chips):
             sent(p_strip(l, row), pf_send.at[l, d])
@@ -379,8 +411,14 @@
 
         @pl.when(layer == l)
         def _():
+            for side in sides(l):
+                sent(pl_piece(l, row), plz_send.at[l, side])
+                sent(p_strip(l, row), pz_send.at[l, side])
+            for source in sources(l):
+                for side in sides(l, source):
+                    sent(pl_piece(source, row), plz_send.at[source, side])
+                    sent(p_strip(source, row), pz_send.at[source, side])
             for d in range(1, layers):
-                sent(p_strip(l, row), pz_send.at[d])
                 for s in range(count[l]):
                     sent(mall.at[first[l] + s], m_send.at[first[l] + s, d])
 
@@ -397,7 +435,7 @@
     tiles, _, rank, width = tile_left.shape
     slots = max(owners(tiles, layers)[0])
     dma = pltpu.SemaphoreType.DMA
-    hbm = pl.BlockSpec(memory_space=pl.ANY)
+    hbm = pl.BlockSpec(memory_space=pltpu.HBM)
     lanes = (layers + 2) * rank
     return pl.pallas_call(
         partial(kernel, layers, rows),
@@ -417,20 +455,20 @@
             pltpu.VMEM((2, width, width), BF16),
             pltpu.VMEM((tiles * rank, width), F32),
             pltpu.VMEM((tiles, rank, width), BF16),
-            pltpu.VMEM((tiles, rank, width), BF16),
+            pltpu.VMEM((tiles, 2, rank, width), BF16),
             pltpu.VMEM((rank, width), BF16),
             pltpu.VMEM((tiles, rank, width), F32),
             dma((rows,)), dma((rows,)), dma((rows,)), dma((layers, rows)),
-            dma((layers,)), dma((layers, rows)), dma((layers, rows)), dma((layers, rows)),
-            dma((layers,)), dma((layers, rows)),
+            dma((layers, 2)), dma((layers, rows)), dma((layers, rows)), dma((layers, rows)),
+            dma((layers, 2)), dma((layers, rows)),
             dma((tiles,)), dma((slots, layers)), dma((tiles,)), dma((slots, layers)),
-            dma((tiles, layers)), dma((tiles,)), dma((6,)), dma((2, slots)), dma((width // 256,)),
+            dma((tiles, layers)), dma((tiles,)), dma((7,)), dma((2, slots)), dma((width // 256,)),
         ],
         compiler_params=pltpu.CompilerParams(
-            collective_id=0, has_side_effects=True, vmem_limit_bytes=50 * 1024 * 1024
+            collective_id=0, has_side_effects=True, vmem_limit_bytes=63 * 1024 * 1024
         ),
     )(
-        tile_mask, tile_left.reshape(tiles, rank, width), tile_right.reshape(tiles, rank, width),
+        tile_mask.reshape(tiles), tile_left.reshape(tiles, rank, width), tile_right.reshape(tiles, rank, width),
         orig_left, orig_right, pivot_left.reshape(rank, -1), pivot_right.reshape(rank, -1),
         sketch, pivot_factor,
     )

time: 72.5 us -> 69.3 us (0.956)
  the two profiles are of different devices: /device:TPU:25 before, /device:TPU:1 now
where the time goes in v3:
time: 69.3 us; the launch traced here: 69.2 us
  Pallas kernels  66.4 us (96%)
  local copies, waits for them, and re-layouts  2.73 us (4%)
    pallas_call x1, Pallas kernels, shards_kernel(): pl.pallas_call(partial(kernel, layers, rows), out_shape=jax.ShapeDtypeStr...  66.4 us
    unnamed x1, local copies, waits for them, and re-layouts  2.73 us

profile of v3, /device:TPU:1, one launch (start us, length us, event | category | flops | bytes accessed | tf_op | source)
XLA Modules:
  0.0 69.2 jit_solution(4665093276593775759)
XLA Ops:
  0.0 66.4 %shard_map.91 = f32[6,64,1024]{2,1,0:T(8,128)} custom-call(s32[6]{0:T(128)} %bitcast.9, bf16[6,64,1024]{2,1,0:T(8,128)(2,1)} %bitcast.5, bf16[6,64,1024]{2,1,0:T(8,128)(2,1)} %bitcast.6, bf16[6,64,1024]{2,1,0:T(8,128)(2,1)} %ol_ref.1, bf16[6,64,1024]{2,1,0:T(8,128)(2,1)} %or_ref.1, bf16[64,128]{1,0:T(8,128)(2,1)} %bitcast.7, bf16[64,128]{1,0:T(8,128)(2,1)} %bitcast.8, ...), custom_call_target="tpu_custom_call" | custom-call | tf_op jit(solution)/shard_map/pallas_call | solution.py:440
  66.4 2.7 %copy.11 = f32[6,64,1024]{2,1,0:T(8,128)} copy(f32[6,64,1024]{2,1,0:T(8,128)} %shard_map.91) | data formatting | bytes 3145728

commit v4 on v3

--- a/solution.py
+++ b/solution.py
@@ -153,17 +153,20 @@
         start = pl.multiple_of((l * rows + r) * strip, strip)
         return pw.at[pl.ds(start, strip), pl.ds(0, used(l))]
 
-    def sides(l, source=None):
-        both = [side for side in (0, 1) if 0 <= l + 2 * side - 1 < layers]
-        if source is None:
-            return both
-        return [side for side in both if side == (source < l)]
-
     def sources(l):
         return sorted((i for i in range(layers) if i != l), key=lambda i: (abs(i - l), i))
 
     def own_strip(l):
         return pf_ref.at[:, pl.ds(0, used(l))]
+
+    def share_strips(l):
+        for d in range(chips):
+            r = other_row(2 * d)
+            if d:
+                here(p_strip(l, r), p_recv.at[l, r])
+            send(
+                p_strip(l, r), p_strip(l, r), p3_send.at[l, d], p_recv.at[l, r], to(layer, sibling)
+            ).start()
 
     barrier = pltpu.get_barrier_semaphore()
     for d in range(1, layers):
@@ -197,18 +200,14 @@
             pl_ref, pl_piece(layer, row), pl_send.at[d], pl_recv.at[layer, row],
             to(layer, other_row(d)),
         ).start()
+    for d in range(1, layers):
+        send(
+            pl_ref, pl_piece(layer, row), plz_send.at[d], pl_recv.at[layer, row], to(other_layer(d), row)
+        ).start()
     for l in range(layers):
 
         @pl.when(layer == l)
         def _():
-            for side in sides(l):
-                send(
-                    pl_ref, pl_piece(l, row), plz_send.at[l, side], pl_recv.at[l, row], to(l + 2 * side - 1, row)
-                ).start()
-                send(
-                    own_strip(l), p_strip(l, row), pz_send.at[l, side], p_recv.at[l, row],
-                    to(l + 2 * side - 1, row),
-                ).start()
             for d in range(1, chips):
                 send(
                     own_strip(l), p_strip(l, row), pf_send.at[l, d], p_recv.at[l, row],
@@ -267,26 +266,19 @@
         def _():
             for l in sources(me):
                 here(pl_piece(l, row), pl_recv.at[l, row])
-                here(p_strip(l, row), p_recv.at[l, row])
-                for side in sides(me, l):
-                    send(
-                        pl_piece(l, row), pl_piece(l, row), plz_send.at[l, side], pl_recv.at[l, row],
-                        to(me + 2 * side - 1, row),
-                    ).start()
-                    send(
-                        p_strip(l, row), p_strip(l, row), pz_send.at[l, side], p_recv.at[l, row],
-                        to(me + 2 * side - 1, row),
-                    ).start()
                 for d in range(1, rows):
                     send(
                         pl_piece(l, row), pl_piece(l, row), plf_send.at[l, d], pl_recv.at[l, row],
                         to(layer, other_row(d)),
                     ).start()
-                for d in range(1, chips):
-                    send(
-                        p_strip(l, row), p_strip(l, row), pf_send.at[l, d], p_recv.at[l, row],
-                        to(layer, other_row(2 * d)),
-                    ).start()
+            share_strips(me)
+            for l in range(layers):
+                for s in range(count[l] if l != me else 0):
+                    sent(tl_ref.at[first[l] + s], tl_send.at[first[l] + s])
+            for l in reversed(sources(me)):
+                send(
+                    own_strip(me), p_strip(me, row), pz_send.at[l], p_recv.at[me, row], to(l, row)
+                ).start()
 
     for l in range(layers):
 
@@ -326,14 +318,19 @@
                         mall.at[t], mall.at[t], m_send.at[t, d], m_recv.at[t], to(other_layer(d), row)
                     ).start()
 
-    for d in range(chips):
-        for l in range(layers):
-            r = other_row(2 * d)
-            if d:
-                here(p_strip(l, r), p_recv.at[l, r])
-            send(
-                p_strip(l, r), p_strip(l, r), p3_send.at[l, d], p_recv.at[l, r], to(layer, sibling)
-            ).start()
+    for me in range(layers):
+
+        @pl.when(layer == me)
+        def _():
+            for l in sources(me):
+                here(p_strip(l, row), p_recv.at[l, row])
+                for d in range(1, chips):
+                    send(
+                        p_strip(l, row), p_strip(l, row), pf_send.at[l, d], p_recv.at[l, row],
+                        to(layer, other_row(2 * d)),
+                    ).start()
+            for l in sources(me):
+                share_strips(l)
 
     for l in range(layers):
         for d in range(chips):
@@ -403,6 +400,8 @@
     for d in range(1, rows):
         sent(pr_piece(row), pr_send.at[d])
         sent(pl_piece(layer, row), pl_send.at[d])
+    for d in range(1, layers):
+        sent(pl_piece(layer, row), plz_send.at[d])
     for l in range(layers):
         for d in range(1, chips):
             sent(p_strip(l, row), pf_send.at[l, d])
@@ -411,13 +410,8 @@
 
         @pl.when(layer == l)
         def _():
-            for side in sides(l):
-                sent(pl_piece(l, row), plz_send.at[l, side])
-                sent(p_strip(l, row), pz_send.at[l, side])
-            for source in sources(l):
-                for side in sides(l, source):
-                    sent(pl_piece(source, row), plz_send.at[source, side])
-                    sent(p_strip(source, row), pz_send.at[source, side])
+            for other in sources(l):
+                sent(p_strip(l, row), pz_send.at[other])
             for d in range(1, layers):
                 for s in range(count[l]):
                     sent(mall.at[first[l] + s], m_send.at[first[l] + s, d])
@@ -427,7 +421,6 @@
             for d in range(1, rows):
                 sent(pl_piece(l, row), plf_send.at[l, d])
             for s in range(count[l]):
-                sent(tl_ref.at[first[l] + s], tl_send.at[first[l] + s])
                 sent(ce.at[first[l] + s], ce_send.at[first[l] + s])
 
 
@@ -459,8 +452,8 @@
             pltpu.VMEM((rank, width), BF16),
             pltpu.VMEM((tiles, rank, width), F32),
             dma((rows,)), dma((rows,)), dma((rows,)), dma((layers, rows)),
-            dma((layers, 2)), dma((layers, rows)), dma((layers, rows)), dma((layers, rows)),
-            dma((layers, 2)), dma((layers, rows)),
+            dma((layers,)), dma((layers, rows)), dma((layers, rows)), dma((layers, rows)),
+            dma((layers,)), dma((layers, rows)),
             dma((tiles,)), dma((slots, layers)), dma((tiles,)), dma((slots, layers)),
             dma((tiles, layers)), dma((tiles,)), dma((7,)), dma((2, slots)), dma((width // 256,)),
         ],

time: 69.3 us -> 71.8 us (1.036)
  Pallas kernels: 66.4 us -> 68.7 us
    pallas_call x1, Pallas kernels: 66.4 us -> 68.7 us  [shards_kernel(): pl.pallas_call(partial(kernel, layers, rows), out_shape=jax.ShapeDtypeStr...]
where the time goes in v4:
time: 71.8 us; the launch traced here: 71.4 us
  Pallas kernels  68.7 us (96%)
  local copies, waits for them, and re-layouts  2.73 us (4%)
    pallas_call x1, Pallas kernels, shards_kernel(): pl.pallas_call(partial(kernel, layers, rows), out_shape=jax.ShapeDtypeStr...  68.7 us
    unnamed x1, local copies, waits for them, and re-layouts  2.73 us

profile of v4, /device:TPU:1, one launch (start us, length us, event | category | flops | bytes accessed | tf_op | source)
XLA Modules:
  0.0 71.4 jit_solution(16755734940761133989)
XLA Ops:
  0.0 68.7 %shard_map.91 = f32[6,64,1024]{2,1,0:T(8,128)} custom-call(s32[6]{0:T(128)} %bitcast.9, bf16[6,64,1024]{2,1,0:T(8,128)(2,1)} %bitcast.5, bf16[6,64,1024]{2,1,0:T(8,128)(2,1)} %bitcast.6, bf16[6,64,1024]{2,1,0:T(8,128)(2,1)} %ol_ref.1, bf16[6,64,1024]{2,1,0:T(8,128)(2,1)} %or_ref.1, bf16[64,128]{1,0:T(8,128)(2,1)} %bitcast.7, bf16[64,128]{1,0:T(8,128)(2,1)} %bitcast.8, ...), custom_call_target="tpu_custom_call" | custom-call | tf_op jit(solution)/shard_map/pallas_call | solution.py:433
  68.7 2.7 %copy.11 = f32[6,64,1024]{2,1,0:T(8,128)} copy(f32[6,64,1024]{2,1,0:T(8,128)} %shard_map.91) | data formatting | bytes 3145728

commit v5 on v4

--- a/solution.py
+++ b/solution.py
@@ -208,6 +208,10 @@
 
         @pl.when(layer == l)
         def _():
+            for other in reversed(sources(l)):
+                send(
+                    own_strip(l), p_strip(l, row), pz_send.at[other], p_recv.at[l, row], to(other, row)
+                ).start()
             for d in range(1, chips):
                 send(
                     own_strip(l), p_strip(l, row), pf_send.at[l, d], p_recv.at[l, row],
@@ -271,14 +275,13 @@
                         pl_piece(l, row), pl_piece(l, row), plf_send.at[l, d], pl_recv.at[l, row],
                         to(layer, other_row(d)),
                     ).start()
+                here(p_strip(l, row), p_recv.at[l, row])
+                for d in range(1, chips):
+                    send(
+                        p_strip(l, row), p_strip(l, row), pf_send.at[l, d], p_recv.at[l, row],
+                        to(layer, other_row(2 * d)),
+                    ).start()
             share_strips(me)
-            for l in range(layers):
-                for s in range(count[l] if l != me else 0):
-                    sent(tl_ref.at[first[l] + s], tl_send.at[first[l] + s])
-            for l in reversed(sources(me)):
-                send(
-                    own_strip(me), p_strip(me, row), pz_send.at[l], p_recv.at[me, row], to(l, row)
-                ).start()
 
     for l in range(layers):
 
@@ -322,13 +325,6 @@
 
         @pl.when(layer == me)
         def _():
-            for l in sources(me):
-                here(p_strip(l, row), p_recv.at[l, row])
-                for d in range(1, chips):
-                    send(
-                        p_strip(l, row), p_strip(l, row), pf_send.at[l, d], p_recv.at[l, row],
-                        to(layer, other_row(2 * d)),
-                    ).start()
             for l in sources(me):
                 share_strips(l)
 
@@ -421,6 +417,7 @@
             for d in range(1, rows):
                 sent(pl_piece(l, row), plf_send.at[l, d])
             for s in range(count[l]):
+                sent(tl_ref.at[first[l] + s], tl_send.at[first[l] + s])
                 sent(ce.at[first[l] + s], ce_send.at[first[l] + s])
 
 

time: 71.8 us -> 63.9 us (0.89)
  Pallas kernels: 68.7 us -> 61 us
    pallas_call x1, Pallas kernels: 68.7 us -> 61 us  [shards_kernel(): pl.pallas_call(partial(kernel, layers, rows), out_shape=jax.ShapeDtypeStr...]
where the time goes in v5:
time: 63.9 us; the launch traced here: 63.8 us
  Pallas kernels  61 us (95%)
  local copies, waits for them, and re-layouts  2.73 us (4%)
    pallas_call x1, Pallas kernels, shards_kernel(): pl.pallas_call(partial(kernel, layers, rows), out_shape=jax.ShapeDtypeStr...  61 us
    unnamed x1, local copies, waits for them, and re-layouts  2.73 us

profile of v5, /device:TPU:1, one launch (start us, length us, event | category | flops | bytes accessed | tf_op | source)
XLA Modules:
  0.0 63.8 jit_solution(308230055992566461)
XLA Ops:
  0.0 61.0 %shard_map.91 = f32[6,64,1024]{2,1,0:T(8,128)} custom-call(s32[6]{0:T(128)} %bitcast.9, bf16[6,64,1024]{2,1,0:T(8,128)(2,1)} %bitcast.5, bf16[6,64,1024]{2,1,0:T(8,128)(2,1)} %bitcast.6, bf16[6,64,1024]{2,1,0:T(8,128)(2,1)} %ol_ref.1, bf16[6,64,1024]{2,1,0:T(8,128)(2,1)} %or_ref.1, bf16[64,128]{1,0:T(8,128)(2,1)} %bitcast.7, bf16[64,128]{1,0:T(8,128)(2,1)} %bitcast.8, ...), custom_call_target="tpu_custom_call" | custom-call | tf_op jit(solution)/shard_map/pallas_call | solution.py:430
  61.0 2.7 %copy.11 = f32[6,64,1024]{2,1,0:T(8,128)} copy(f32[6,64,1024]{2,1,0:T(8,128)} %shard_map.91) | data formatting | bytes 3145728
